TPU v7x, 32 devices: a whole 2x2x4 slice. The times are simulated.
32 devices in a mesh: groups: 2 (over x), ctx: 8 (over z, y), head: 2 (over core).
Axes of the slice: x: 2, y: 2, z: 4, core: 2. Of those that a mesh axis runs over, the one named last changes fastest.
Arguments:
- q_prefill: bfloat16 [2048, 64, 576], P(('groups', 'ctx'), 'head'), parts along dimension 0, may hold values from -300 to 300
- kv_raw: bfloat16 [2048, 576], P(('groups', 'ctx')), parts along dimension 0, may hold values from -6 to 6
- kv_gain: float32 [512], replicated, may hold values from 0.1 to 1.9
- block_mask: int32 [16, 8], P('groups'), parts along dimension 0, may hold values from 0 to 1, as said below
- owner: int32 [16], P('groups'), parts along dimension 0, may hold values from 0 to 7, as said below
- decode_len: int32 [32], P('groups'), parts along dimension 0, may hold values from 1 to 1024, as said below
- q_decode: bfloat16 [3, 32, 64, 576], P(None, 'groups', 'head'), parts along dimension 1, may hold values from -300 to 300
- kv_new_raw: bfloat16 [3, 32, 576], P(None, 'groups'), parts along dimension 1, may hold values from -6 to 6
Outputs:
- prefill_out: bfloat16 [2048, 64, 512], P(('groups', 'ctx'), 'head'), parts along dimension 0
- owner_cache: bfloat16 [32, 128, 576], P(('groups', 'ctx')), parts along dimension 0
- decode_out: bfloat16 [3, 32, 64, 512], P(None, 'groups', 'head'), parts along dimension 1
There are 2 independent parts, one for each index of `groups`. A program takes and returns all parts, laid end to end along the dimension named above; an argument that names none is the same for every part. Nothing has to cross between parts.
Inputs may be any that keep to these rules, and one draw needn't show every extreme that they name: block_mask[i, j] is 0 for j > i, and 1 for j = i, for j = i - 1 and for j = 0. No owner holds more than 2 blocks; some owner holds exactly 2. `decode_len`: some row reads exactly 1024 prompt rows.
All inputs are finite; a program needn't handle non-finite values.
Results may differ from a plain program's by a relative error of at most 0.005.
The roundings to bfloat16 on the way count: a program that leaves them out, or rounds other values in their place, can miss the bound.
Values may be sent and summed in bfloat16 or wider, within the bound.
A program may use at most 128 MiB of HBM per device.

v0:
```python
from functools import partial

import jax
import jax.numpy as jnp
from jax import lax
from jax.sharding import PartitionSpec as P

BLK = 128
CAP = 2


scale_factor = 192.0 ** (-0.5)
neg_large = -1e30


def normalize_latent(raw_rows, gain_vector, positions):
    values = raw_rows.astype(jnp.float32)
    latent_width = gain_vector.shape[0]
    main_part = values[..., :latent_width]
    main_part = (
        main_part
        * lax.rsqrt(jnp.mean(main_part * main_part, axis=-1, keepdims=True) + 1e-06)
        * gain_vector
    )
    rotary = values[..., latent_width:]
    half_width = rotary.shape[-1] // 2
    frequency = 10000.0 ** (-2.0 * jnp.arange(half_width, dtype=jnp.float32) / rotary.shape[-1])
    angles = positions.astype(jnp.float32)[..., None] * frequency
    cosine = jnp.cos(angles)
    sine_part = jnp.sin(angles)
    first_half = rotary[..., :half_width]
    second_half = rotary[..., half_width:]
    joined = jnp.concatenate(
        [
            main_part,
            first_half * cosine - second_half * sine_part,
            first_half * sine_part + second_half * cosine,
        ],
        axis=-1,
    )
    return joined.astype(jnp.bfloat16)


def keep_state(state_now):
    return state_now


def body(q_prefill, kv_raw, kv_gain, block_mask, owner, decode_len, q_decode, kv_new_raw):
    row_count = q_prefill.shape[0]
    heads_here = q_prefill.shape[1]
    latent_width = kv_gain.shape[0]
    full_width = kv_raw.shape[1]
    my_index = lax.axis_index("ctx")
    positions = my_index * row_count + jnp.arange(row_count, dtype=jnp.int32)
    latent = normalize_latent(kv_raw, kv_gain, positions)
    query_blocks = row_count // BLK
    my_blocks = my_index * query_blocks + jnp.arange(query_blocks, dtype=jnp.int32)
    my_mask = lax.dynamic_slice_in_dim(block_mask, my_index * query_blocks, query_blocks, 0)

    def absorb(key_rows, key_block, block_live, carried):
        running_max, running_sum, weighted = carried
        row_live = jnp.broadcast_to(block_live[:, None], (query_blocks, BLK)).reshape(row_count)
        key_pos = key_block * BLK + jnp.arange(BLK, dtype=jnp.int32)
        allowed = row_live[:, None] & (key_pos[None, :] <= positions[:, None])
        scores = (
            jnp.einsum("thc,sc->ths", q_prefill, key_rows, preferred_element_type=jnp.float32)
            * scale_factor
        )
        scores = jnp.where(allowed[:, None, :], scores, neg_large)
        new_max = jnp.maximum(running_max, jnp.max(scores, axis=-1))
        weights = jnp.where(allowed[:, None, :], jnp.exp(scores - new_max[..., None]), 0.0)
        factor = jnp.exp(running_max - new_max)
        running_sum = running_sum * factor + jnp.sum(weights, axis=-1)
        weighted = weighted * factor[..., None] + jnp.einsum(
            "ths,sc->thc",
            weights.astype(jnp.bfloat16),
            key_rows[:, :latent_width],
            preferred_element_type=jnp.float32,
        )
        return (new_max, running_sum, weighted)

    block_count = owner.shape[0]
    owned = owner == my_index
    rank = jnp.cumsum(owned.astype(jnp.int32)) - 1
    pick = owned[None, :] & (rank[None, :] == jnp.arange(CAP, dtype=jnp.int32)[:, None])
    block_ids = jnp.sum(
        jnp.where(pick, jnp.arange(block_count, dtype=jnp.int32)[None, :], 0), axis=1
    )
    slot_live = jnp.any(pick, axis=1)
    start_state = (
        jnp.full((row_count, heads_here), neg_large, jnp.float32),
        jnp.zeros((row_count, heads_here), jnp.float32),
        jnp.zeros((row_count, heads_here, latent_width), jnp.float32),
    )
    gathered = lax.all_gather(latent, "ctx", axis=0, tiled=True)
    block_total = gathered.shape[0] // BLK

    def visit_block(inner_step, inner):
        key_block = 0 // BLK + inner_step
        key_rows = lax.dynamic_slice_in_dim(gathered, inner_step * BLK, BLK, 0)
        block_live = (lax.dynamic_slice_in_dim(my_mask, key_block, 1, 1)[:, 0] == 1) & (
            key_block <= my_blocks
        )
        return lax.cond(
            jnp.any(block_live), partial(absorb, key_rows, key_block, block_live), keep_state, inner
        )

    final_state = lax.fori_loop(0, block_total, visit_block, start_state)
    owner_cache = jnp.where(
        slot_live[:, None, None],
        gathered.reshape(block_count, BLK, full_width)[block_ids],
        jnp.zeros((), jnp.bfloat16),
    )
    prefill_out = (final_state[2] / final_state[1][..., None]).astype(jnp.bfloat16)
    cache_rows = owner_cache.reshape(CAP * BLK, full_width)
    key_pos = (block_ids[:, None] * BLK + jnp.arange(BLK, dtype=jnp.int32)[None, :]).reshape(
        CAP * BLK
    )
    key_live = jnp.broadcast_to(slot_live[:, None], (CAP, BLK)).reshape(CAP * BLK)
    cache_valid = key_live[None, :] & (key_pos[None, :] < decode_len[:, None])
    scores = (
        jnp.einsum("srhc,kc->srhk", q_decode, cache_rows, preferred_element_type=jnp.float32)
        * scale_factor
    )
    scores = jnp.where(cache_valid[None, :, None, :], scores, neg_large)
    local_max = jnp.max(scores, axis=-1)
    cache_top = lax.pmax(local_max, "ctx")
    weights = jnp.where(cache_valid[None, :, None, :], jnp.exp(scores - cache_top[..., None]), 0.0)
    local_weighted = jnp.einsum(
        "srhk,kc->srhc",
        weights.astype(jnp.bfloat16),
        cache_rows[:, :latent_width],
        preferred_element_type=jnp.float32,
    )
    cache_weighted, cache_total = lax.psum((local_weighted, jnp.sum(weights, axis=-1)), "ctx")
    step_count = q_decode.shape[0]
    new_pos = decode_len[None, :] + jnp.arange(step_count, dtype=jnp.int32)[:, None]
    new_latent = normalize_latent(kv_new_raw, kv_gain, new_pos)
    new_scores = (
        jnp.einsum("srhc,jrc->srhj", q_decode, new_latent, preferred_element_type=jnp.float32)
        * scale_factor
    )
    new_valid = jnp.arange(step_count)[None, :] <= jnp.arange(step_count)[:, None]
    new_scores = jnp.where(new_valid[:, None, None, :], new_scores, neg_large)
    final_top = jnp.maximum(cache_top, jnp.max(new_scores, axis=-1))
    factor = jnp.exp(cache_top - final_top)
    new_weights = jnp.where(
        new_valid[:, None, None, :], jnp.exp(new_scores - final_top[..., None]), 0.0
    )
    total = cache_total * factor + jnp.sum(new_weights, axis=-1)
    weighted = cache_weighted * factor[..., None] + jnp.einsum(
        "srhj,jrc->srhc",
        new_weights.astype(jnp.bfloat16),
        new_latent[..., :latent_width],
        preferred_element_type=jnp.float32,
    )
    decode_out = (weighted / total[..., None]).astype(jnp.bfloat16)
    return (prefill_out, owner_cache, decode_out)


def solution(mesh):
    return jax.shard_map(
        body,
        mesh=mesh,
        in_specs=(
            P(("groups", "ctx"), "head", None),
            P(("groups", "ctx"), None),
            P(),
            P("groups", None),
            P("groups"),
            P("groups"),
            P(None, "groups", "head", None),
            P(None, "groups", None),
        ),
        out_specs=(
            P(("groups", "ctx"), "head", None),
            P(("groups", "ctx"), None, None),
            P(None, "groups", "head", None),
        ),
        check_vma=False,
    )
```

profile of v0, /device:TPU:2, one launch (start us, length us, event | category | flops | bytes accessed | tf_op | source)
XLA Modules:
  0.0 254.9 jit_solution(1596706416954336392)
XLA Ops:
  7.2 0.0 all-gather.2.cloned.1.call-start
  7.3 1.1 convert_element_type.50
  8.3 0.1 multiply_reduce_fusion
  8.4 0.1 fusion.52
  8.6 0.8 multiply_convert_fusion
  9.4 0.7 pad_maximum_fusion
  10.1 0.0 all-reduce.2.cloned.1.call-start
  10.1 0.7 convert_bitcast_fusion
  10.8 0.2 reduce-window.8
  11.0 0.8 convert_element_type.54
  11.9 0.1 select_reduce_fusion
  12.0 0.1 fusion.55
  12.1 0.1 multiply_reduce_fusion.1
  12.2 0.1 broadcast_bitcast_fusion
  12.3 0.1 add_bitcast_fusion
  12.4 0.7 add_convert_fusion
  13.0 0.7 compare_and_fusion.1
  13.8 39.1 %all-gather.2.cloned.1.call-done = bf16[1024,576]{0,1:T(8,128)(2,1)} async-done(((bf16[128,576]{0,1:T(8,128)(2,1)}), bf16[1024,576]{0,1:T(8,128)(2,1)}) %all-gather.2.cloned.1.call-update) | async-done | bytes 1179664 | tf_op jit(solution)/shard_map/all_gather | solution.py:95
  52.8 1.5 copy_bitcast_fusion
  54.3 0.6 gather_fusion
  55.0 0.2 copy.86
  55.2 0.5 copy-done.3
  55.7 0.1 bitcast_select_fusion.2
  55.8 1.5 fusion.59
  57.3 36.3 %pmax.7 = f32[3,16,32]{2,1,0:T(8,128)} all-reduce(f32[3,16,32]{2,1,0:T(8,128)} %get-tuple-element.317), channel_id=1, replica_groups=mesh['groups'=2,'ctx'=8,'head'=2] {'ctx'}, use_global_device_ids=true, to_apply=%region_11.12 | all-reduce | flops 1536 | bytes 12288 | tf_op jit(solution)/shard_map/pmax | solution.py:127
  93.6 3.3 %fusion.26 = f32[3,16,32,512]{3,2,1,0:T(8,128)} fusion(f32[3,16,32,256]{3,2,1,0:T(8,128)S(1)} %get-tuple-element.318, f32[3,16,32]{2,1,0:T(8,128)} %pmax.7, pred[16,256]{1,0:T(8,128)(4,1)S(1)} %compare_and_fusion.1, bf16[256,576]{1,0:T(8,128)(2,1)} %copy-done.5), kind=kOutput, calls=%fused_computation.40 | convolution fusion | flops 403832832 | bytes 5009408 | tf_op jit(solution)/shard_map/srhk,kc->srhc/dot_general | solution.py:129
  97.0 1.3 constant_dynamic-slice_fusion.1
  98.3 1.0 fusion.43
  99.2 1.0 multiply_convert_fusion.1
  100.3 0.6 copy-done.7
  100.9 0.1 maximum_bitcast_fusion
  101.0 1.3 fusion.22
  102.3 0.7 copy-done.6
  102.9 0.7 fusion.46
  103.6 0.6 broadcast_in_dim.148
  104.2 0.6 broadcast_in_dim.149
  104.8 4.3 %broadcast_in_dim.150 = f32[128,32,512]{2,0,1:T(8,128)} broadcast(f32[]{:T(128)} %constant.112.clone.1), dimensions={} | broadcast | bytes 8388612 | tf_op jit(solution)/shard_map/broadcast_in_dim | solution.py:93
  109.1 29.9 %while.18 = (s32[]{:T(128)}, f32[128,32]{0,1:T(8,128)}, f32[128,32]{0,1:T(8,128)}, f32[128,32,512]{2,0,1:T(8,128)}, s32[1,8]{1,0:T(1,128)}, /*index=5*/s32[1]{0:...) while((s32[]{:T(128)}, f32[128,32]{0,1:T(8,128)}, ...), condition=%wide.region_6.7_spmd.clone, body=%wide.region_1.6_spmd.clone.sunk | while | flops 1151901952 | bytes 95505792 | solution.py:108
  109.1 1.3 fusion.64
  111.0 14.4 %conditional.3 = ((f32[128,32]{0,1:T(8,128)}, f32[128,32]{0,1:T(8,128)}, f32[128,32,512]{2,0,1:T(8,128)})) conditional(s32[]{:T(128)} %bitcast.81, (f32[128,32]{0,1:T(8,128)}, f32[128,32]{0,1:T(8,128)}, f32[128,32,512]{2,0,1:T(8,128)}) %tuple.62, (pred[1]{0:T(512)(128)(4,1)}, s32[]{:T(128)}, s32[]{:T(128)}, bf16[1024,576]{0,1:T(8,128)(2,1)}, ...), branch_computations={%region_2.2_spmd, %region_3.5_spmd} | conditional | flops 1151901952 | bytes 95505048 | solution.py:104
  111.1 0.1 compare_and_fusion
  111.2 3.6 %fusion.2 = (f32[128,32]{0,1:T(8,128)S(1)}, f32[128,128,32]{1,0,2:T(8,128)S(1)}) fusion(pred[128,128]{0,1:T(8,128)(4,1)S(1)} %compare_and_fusion, bf16[128,32,576]{0,2,1:T(8,128)(2,1)} %get-tuple-element.233, bf16[1024,576]{0,1:T(8,128)(2,1)} %get-tuple-element.232, s32[]{:T(128)S(6)} %select_n.52), kind=kOutput, calls=%fused_computation.5 | convolution fusion | flops 605548544 | bytes 6995972 | tf_op jit(solution)/shard_map/while/body/eval_jaxpr/cond/branch_1_fun/thc,sc->ths/dot_general | solution.py:66
  114.8 1.0 max.8
  115.8 0.6 fusion.4
  116.4 1.4 multiply_add_fusion.1
  117.7 0.6 copy.135
  118.3 3.9 %multiply_add_fusion = f32[128,32,512]{2,0,1:T(8,128)S(1)} fusion(f32[128,32,512]{2,0,1:T(8,128)S(1)} %copy-done.1, f32[128,32]{0,1:T(8,128)S(1)} %get-tuple-element.302, f32[128,128,32]{1,0,2:T(8,128)S(1)} %get-tuple-element.308, f32[128,32]{0,1:T(8,128)S(1)} %max.8, pred[128,128]{0,1:T(8,128)(4,1)S(1)} %compare_and_fusion, ...), kind=kOutput, calls=%fused_computation.2 | convolution fusion | flops 543686656 | bytes 19054596 | tf_op jit(solution)/shard_map/while/body/eval_jaxpr/cond/branch_1_fun/ths,sc->thc/dot_general | solution.py:74
  122.2 3.2 %copy-done.2 = f32[128,32,512]{2,0,1:T(8,128)} copy-done((f32[128,32,512]{2,0,1:T(8,128)}, f32[128,32,512]{2,0,1:T(8,128)S(1)}, u32[]{:S(2)}) %copy-start.2) | copy-done | bytes 8388632 | tf_op jit(solution)/shard_map/while/body/eval_jaxpr/cond
  125.4 1.3 fusion.64
  127.4 1.3 fusion.64
  129.3 1.3 fusion.64
  131.3 1.3 fusion.64
  133.2 1.3 fusion.64
  135.2 1.3 fusion.64
  137.1 1.3 fusion.64
  139.1 1.4 copy.83
  140.5 1.4 max.10
  141.9 1.9 fusion.24
  143.7 87.5 %psum.15 = f32[3,16,32]{2,1,0:T(8,128)S(1)} all-reduce(f32[3,16,32]{2,1,0:T(8,128)} %fusion.24), channel_id=1, replica_groups=mesh['groups'=2,'ctx'=8,'head'=2] {'ctx'}, use_global_device_ids=true, to_apply=%region_16.17 | all-reduce | flops 1536 | bytes 12288 | tf_op jit(solution)/shard_map/psum | solution.py:135
  231.2 1.0 fusion.36
  232.2 0.8 multiply_add_fusion.2
  233.0 1.8 broadcast_select_fusion
  234.8 10.1 %fusion.19 = bf16[128,32,512]{2,1,0:T(8,128)(2,1)} fusion(f32[128,32,512]{2,0,1:T(8,128)} %get-tuple-element.254, f32[128,32]{1,0:T(8,128)} %copy.83), kind=kLoop, calls=%fused_computation.29 | loop fusion | flops 4194304 | bytes 12599296 | tf_op jit(solution)/shard_map/convert_element_type | solution.py:114
  244.9 3.2 %fusion.21 = bf16[3,16,32,512]{3,2,1,0:T(8,128)(2,1)} fusion(f32[3,16,32,512]{3,2,1,0:T(8,128)} %all-reduce.2.cloned.1.call-done, f32[3,16,32]{2,1,0:T(8,128)S(1)} %get-tuple-element.303, f32[3,16,32]{2,1,0:T(8,128)S(1)} %get-tuple-element.304, bf16[3,16,512]{2,1,0:T(8,128)(2,1)S(1)} %copy-done.8, bf16[3,16,32,3]{2,1,3,0:T(8,128)(2,1)S(1)} %get-tuple-element.315), kind=kOutput, calls=%fused_computation.32 | convolution fusion | flops 7864320 | bytes 4789248 | tf_op jit(solution)/shard_map/srhj,jrc->srhc/dot_general | solution.py:151
  (54 shorter events, 0.3 us)
Async XLA Ops:
  7.2 48.6 %copy-start = (bf16[3,16,32,576]{3,2,1,0:T(8,128)(2,1)S(1)}, bf16[3,16,32,576]{3,2,1,0:T(8,128)(2,1)}, u32[]{:S(2)}) copy-start(bf16[3,16,32,576]{3,2,1,0:T(8,128)(2,1)} %param.18) | copy-start | bytes 5308420
  7.2 45.7 %all-gather.2.cloned.1.call-start = ((), (), s32[]{:S(2)}) async-start(), calls=%async_computation | async-start | bytes 1327104 | tf_op jit(solution)/shard_map/all_gather | solution.py:95
  7.2 1.2 copy-start.12
  10.1 234.8 %all-reduce.2.cloned.1.call-start = ((), (), s32[]{:S(2)}) async-start(), calls=%async_computation.1 | async-start | bytes 6291456 | tf_op jit(solution)/shard_map/psum | solution.py:135
  11.8 41.0 %copy-start.4 = (f32[3,16,576]{2,1,0:T(8,128)}, f32[3,16,576]{2,1,0:T(8,128)S(1)}, u32[]{:S(2)}) copy-start(f32[3,16,576]{2,1,0:T(8,128)S(1)} %convert_element_type.54) | copy-start | bytes 331780
  12.1 43.1 %copy-start.13 = (pred[2]{0:T(512)(128)(4,1)}, pred[2]{0:T(512)(128)(4,1)S(1)}, u32[]{:S(2)}) copy-start(pred[2]{0:T(512)(128)(4,1)S(1)} %fusion.55) | copy-start | bytes 10
  13.8 79.8 %copy-start.9 = (pred[16,256]{1,0:T(8,128)(4,1)}, pred[16,256]{1,0:T(8,128)(4,1)S(1)}, u32[]{:S(2)}) copy-start(pred[16,256]{1,0:T(8,128)(4,1)S(1)} %compare_and_fusion.1) | copy-start | bytes 12292
  54.9 0.7 copy-start.3
  55.8 1.5 copy-start.5
  96.9 2.3 copy-start.10
  97.0 12.1 %copy-start.11 = (pred[3,3]{1,0:T(4,128)(4,1)}, pred[3,3]{1,0:T(4,128)(4,1)S(1)}, u32[]{:S(2)}) copy-start(pred[3,3]{1,0:T(4,128)(4,1)S(1)} %iota_compare_fusion) | copy-start | bytes 31
  100.3 0.6 copy-start.7
  102.3 0.7 copy-start.6
  111.2 7.2 %copy-start.1 = (f32[128,32,512]{2,0,1:T(8,128)S(1)}, f32[128,32,512]{2,0,1:T(8,128)}, u32[]{:S(2)}) copy-start(f32[128,32,512]{2,0,1:T(8,128)} %get-tuple-element.235) | copy-start | bytes 25165828 | tf_op jit(solution)/shard_map/while/body/eval_jaxpr/cond
  122.2 3.2 %copy-start.2 = (f32[128,32,512]{2,0,1:T(8,128)}, f32[128,32,512]{2,0,1:T(8,128)S(1)}, u32[]{:S(2)}) copy-start(f32[128,32,512]{2,0,1:T(8,128)S(1)} %multiply_add_fusion) | copy-start | bytes 25165828 | tf_op jit(solution)/shard_map/while/body/eval_jaxpr/cond
  139.0 94.0 %copy-start.14 = (pred[2]{0:T(512)(128)(4,1)S(1)}, pred[2]{0:T(512)(128)(4,1)}, u32[]{:S(2)}) copy-start(pred[2]{0:T(512)(128)(4,1)} %copy-done.13) | copy-start | bytes 10
  234.8 10.1 %copy-start.8 = (bf16[3,16,512]{2,1,0:T(8,128)(2,1)S(1)}, bf16[3,16,512]{2,1,0:T(8,128)(2,1)}, u32[]{:S(2)}) copy-start(bf16[3,16,512]{2,1,0:T(8,128)(2,1)} %copy-done.7) | copy-start | bytes 147460
Sparse Core Ops, SparseCore 0:
  10.6 42.1 all-gather.1
  97.1 126.5 all-reduce.1
where the time goes:
time: 260 us; the launch traced here: 255 us
  blocking collectives  124 us (48%)
  other arithmetic  39.2 us (15%)
  waiting for transfers between devices  39.1 us (15%)
  matrix products  16.9 us (6%)
  local copies, waits for them, and re-layouts  16.2 us (6%)
  between operations  14.3 us (6%)
  loops' own time  5.47 us (2%)
    psum x1, blocking collectives, body(): lax.psum((local_weighted, jnp.sum(weights, axis=-1)), 'ctx')  87.5 us
    all_gather x1, waiting for transfers between devices, body(): gathered = lax.all_gather(latent, 'ctx', axis=0, tiled=True)  39.1 us
    pmax x1, blocking collectives, body(): cache_top = lax.pmax(local_max, 'ctx')  36.3 us
    eq x8, other arithmetic, visit_block(): lax.dynamic_slice_in_dim(my_mask, key_block, 1, 1)[:, 0] == 1  10.1 us
    convert_element_type x1, other arithmetic, body(): (final_state[2] / final_state[1][..., None]).astype(jnp.bfloat16)  10.1 us
    another operation x1, loops' own time, body(): final_state = lax.fori_loop(0, block_total, visit_block, start_state)  5.28 us
  transfers between devices with their start and end apart: 2, of which 1 were waited for; matrix products, arithmetic and copies ran while one was open for 21% of the time, Pallas kernels for 0%

commit v1 on v0

v1 whole, which is shorter than its diff:
```python
import functools
import math

import jax
import jax.numpy as jnp
from jax import lax
from jax.experimental import pallas as pl
from jax.experimental.pallas import tpu as pltpu
from jax.sharding import PartitionSpec as P

BLK = 128
CAP = 2
SUB = 256
SPAN = 8

scale_factor = 192.0 ** (-0.5)
exponent_scale = scale_factor * math.log2(math.e)
neg_large = -1e30
VMEM_LIMIT = 56 * 1024 * 1024


def frequencies(half):
    lane = lax.broadcasted_iota(jnp.int32, (1, half), 1).astype(jnp.float32)
    return 10000.0 ** (-2.0 * lane / (2 * half))


def normalize_rows(raw, gain, pos, freq):
    width = gain.shape[1]
    half = (raw.shape[1] - width) // 2
    values = raw.astype(jnp.float32)
    main = values[:, :width]
    mean = jnp.mean(main * main, axis=-1, keepdims=True)
    main = main * lax.rsqrt(mean + 1e-06) * gain
    angles = pos.astype(jnp.float32) * freq
    cosine, sine = jnp.cos(angles), jnp.sin(angles)
    first = values[:, width : width + half]
    second = values[:, width + half :]
    return jnp.concatenate(
        [main, first * cosine - second * sine, first * sine + second * cosine], axis=-1
    ).astype(jnp.bfloat16)


def dot_nt(a, b):
    return lax.dot_general(a, b, (((1,), (1,)), ((), ())), preferred_element_type=jnp.float32)


def dot_nn(a, b):
    return lax.dot_general(a, b, (((1,), (0,)), ((), ())), preferred_element_type=jnp.float32)


def weights_of(scores, top):
    return jnp.exp2((scores - top) * exponent_scale)


def prefill_kernel(mask_ref, q_ref, lat_ref, out_ref, keys_ref, count_ref, *, n_blocks, width):
    step = pl.program_id(0)
    me = lax.axis_index("ctx")
    tokens, heads, full = q_ref.shape
    rows = tokens * heads
    span = min(SPAN, n_blocks)

    @pl.when(step == 0)
    def _():
        if n_blocks > span:
            keys_ref[...] = jnp.zeros_like(keys_ref)
        keys_ref[pl.ds(0, BLK), :] = lat_ref[pl.ds(pl.multiple_of(me * BLK, BLK), BLK), :]

        def place(j, count):
            live = (mask_ref[me, j] == 1) & (j < me)

            @pl.when(live)
            def _():
                keys_ref[pl.ds(pl.multiple_of(count * BLK, BLK), BLK), :] = lat_ref[
                    pl.ds(pl.multiple_of(j * BLK, BLK), BLK), :
                ]

            return count + live.astype(jnp.int32)

        count = lax.fori_loop(0, n_blocks, place, jnp.int32(1))
        count_ref[0] = count

        @pl.when(count < n_blocks)
        def _():
            keys_ref[pl.ds(pl.multiple_of(count * BLK, BLK), BLK), :] = jnp.zeros(
                (BLK, full), keys_ref.dtype
            )

    count = count_ref[0]
    live_keys = count * BLK
    n_sub = rows // SUB
    sub_tokens = SUB // heads

    def load_q(i):
        return q_ref[i * sub_tokens : (i + 1) * sub_tokens].reshape(SUB, full)

    def masked(scores, i, base):
        shape = scores.shape
        column = base + lax.broadcasted_iota(jnp.int32, shape, 1)
        token = step * tokens + i * sub_tokens + lax.broadcasted_iota(jnp.int32, shape, 0) // heads
        limit = jnp.where(column < BLK, token + 1, live_keys)
        return jnp.where(column < limit, scores, neg_large)

    def mask_pairs(scores, i):
        n_keys = scores.shape[1]
        parts = []
        row = lax.broadcasted_iota(jnp.int32, (SUB, BLK), 0) // heads
        column = lax.broadcasted_iota(jnp.int32, (SUB, BLK), 1)
        token = step * tokens + i * sub_tokens + row
        parts.append(jnp.where(column <= token, scores[:, :BLK], neg_large))
        if n_keys > 2 * BLK:
            parts.append(scores[:, BLK : n_keys - BLK])
        last = jnp.where(live_keys == n_keys, 0.0, neg_large)
        parts.append(scores[:, n_keys - BLK :] + last)
        return jnp.concatenate(parts, axis=1)

    def store(i, weighted, total):
        result = weighted * (1.0 / total)
        out_ref[i * sub_tokens : (i + 1) * sub_tokens] = result.astype(out_ref.dtype).reshape(
            sub_tokens, heads, width
        )

    if n_blocks <= span and n_blocks % 2 == 0:
        for pairs in range(1, n_blocks // 2 + 1):
            n_keys = pairs * 2 * BLK

            @pl.when((count + 1) // 2 == pairs)
            def _(n_keys=n_keys):
                scores = dot_nt(load_q(0), keys_ref[:n_keys, :])
                for i in range(n_sub):
                    here = mask_pairs(scores, i)
                    if i + 1 < n_sub:
                        scores = dot_nt(load_q(i + 1), keys_ref[:n_keys, :])
                    top = jnp.max(here, axis=-1, keepdims=True)
                    weights = weights_of(here, top)
                    total = jnp.sum(weights, axis=-1, keepdims=True)
                    weighted = dot_nn(weights.astype(jnp.bfloat16), keys_ref[:n_keys, :width])
                    store(i, weighted, total)

    else:
        chunk = span * BLK
        for i in range(n_sub):
            query = load_q(i)

            def absorb(k, carried, i=i, query=query):
                top, total, weighted = carried
                base = pl.multiple_of(k * chunk, chunk)
                rows_here = keys_ref[pl.ds(base, chunk), :]
                scores = masked(dot_nt(query, rows_here), i, base)
                new_top = jnp.maximum(top, jnp.max(scores, axis=-1, keepdims=True))
                weights = weights_of(scores, new_top)
                factor = weights_of(top, new_top)
                total = total * factor + jnp.sum(weights, axis=-1, keepdims=True)
                weighted = weighted * factor + dot_nn(
                    weights.astype(jnp.bfloat16), rows_here[:, :width]
                )
                return new_top, total, weighted

            start = (
                jnp.full((SUB, 1), neg_large, jnp.float32),
                jnp.zeros((SUB, 1), jnp.float32),
                jnp.zeros((SUB, width), jnp.float32),
            )
            top, total, weighted = lax.fori_loop(0, (count + span - 1) // span, absorb, start)
            store(i, weighted, total)


def prefill(q, gathered, block_mask, width):
    row_count, heads, full = q.shape
    n_blocks = gathered.shape[0] // BLK
    tokens = 32
    return pl.pallas_call(
        functools.partial(prefill_kernel, n_blocks=n_blocks, width=width),
        grid=(row_count // tokens,),
        out_shape=jax.ShapeDtypeStruct((row_count, heads, width), jnp.bfloat16),
        in_specs=[
            pl.BlockSpec(memory_space=pltpu.SMEM),
            pl.BlockSpec((tokens, heads, full), lambda i: (i, 0, 0)),
            pl.BlockSpec(gathered.shape, lambda i: (0, 0)),
        ],
        out_specs=pl.BlockSpec((tokens, heads, width), lambda i: (i, 0, 0)),
        scratch_shapes=[
            pltpu.VMEM(gathered.shape, jnp.bfloat16),
            pltpu.SMEM((1,), jnp.int32),
        ],
        compiler_params=pltpu.CompilerParams(vmem_limit_bytes=VMEM_LIMIT),
        name="prefill",
    )(block_mask, q, gathered)


def decode_kernel(
    owner_ref, len_ref, q_ref, lat_ref, new_ref, gain_ref, out_ref, cache_ref, fresh_ref, *, width
):
    s_step, part = pl.program_id(0), pl.program_id(1)
    me = lax.axis_index("ctx")
    _, r_here, heads, full = q_ref.shape
    n_steps, r_all, _ = new_ref.shape
    n_keys = lat_ref.shape[0]
    n_blocks = n_keys // BLK
    n_new = n_steps * r_all

    @pl.when((s_step == 0) & (part == 0))
    def _():
        cache_ref[...] = jnp.zeros_like(cache_ref)

        def place(b, count):
            mine = owner_ref[b] == me

            @pl.when(mine & (count < CAP))
            def _():
                cache_ref[count] = lat_ref[pl.ds(pl.multiple_of(b * BLK, BLK), BLK), :]

            return count + mine.astype(jnp.int32)

        lax.fori_loop(0, n_blocks, place, jnp.int32(0))
        fresh_ref[...] = jnp.zeros_like(fresh_ref)
        row = lax.broadcasted_iota(jnp.int32, (r_all, 1), 0)
        lens = jnp.zeros((r_all, 1), jnp.int32)
        for r in range(r_all):
            lens = jnp.where(row == r, len_ref[r], lens)
        freq = frequencies((full - width) // 2)
        for s in range(n_steps):
            fresh_ref[s * r_all : (s + 1) * r_all, :] = normalize_rows(
                new_ref[s], gain_ref[...], lens + s, freq
            )

    rows = r_here * heads
    sub_r = SUB // heads
    n_sub = rows // SUB

    def load_q(i):
        return q_ref[0, i * sub_r : (i + 1) * sub_r].reshape(SUB, full)

    def row_limits(i):
        row = lax.broadcasted_iota(jnp.int32, (SUB, 1), 0) // heads
        limit = jnp.zeros((SUB, 1), jnp.int32)
        for k in range(sub_r):
            limit = jnp.where(row == k, len_ref[part * r_here + i * sub_r + k], limit)
        return limit

    def fresh_scores(query, i):
        scores = dot_nt(query, fresh_ref[...])
        column = lax.broadcasted_iota(jnp.int32, scores.shape, 1)
        row = lax.broadcasted_iota(jnp.int32, scores.shape, 0) // heads + part * r_here + i * sub_r
        live = (column % r_all == row) & (column // r_all <= s_step) & (column < n_new)
        return jnp.where(live, scores, neg_large)

    def store(i, weighted, total):
        result = weighted * (1.0 / total)
        out_ref[0, i * sub_r : (i + 1) * sub_r] = result.astype(out_ref.dtype).reshape(
            sub_r, heads, width
        )

    def absorb_fresh(query, i):
        scores = fresh_scores(query, i)
        return scores, jnp.max(scores, axis=-1, keepdims=True)

    def cache_scores(query, limit, base, chunk):
        scores = dot_nt(query, lat_ref[pl.ds(base, chunk), :])
        column = base + lax.broadcasted_iota(jnp.int32, scores.shape, 1)
        return jnp.where(column < limit, scores, neg_large)

    chunk = min(SPAN, n_blocks) * BLK
    for i in range(n_sub):
        query = load_q(i)
        limit = row_limits(i)
        extra, top = absorb_fresh(query, i)
        if n_keys == chunk:
            scores = cache_scores(query, limit, 0, chunk)
            top = jnp.maximum(top, jnp.max(scores, axis=-1, keepdims=True))
            weights = weights_of(scores, top)
            extra = weights_of(extra, top)
            total = jnp.sum(weights, axis=-1, keepdims=True) + jnp.sum(
                extra, axis=-1, keepdims=True
            )
            weighted = dot_nn(weights.astype(jnp.bfloat16), lat_ref[:, :width]) + dot_nn(
                extra.astype(jnp.bfloat16), fresh_ref[:, :width]
            )
        else:
            extra = weights_of(extra, top)
            state = (
                top,
                jnp.sum(extra, axis=-1, keepdims=True),
                dot_nn(extra.astype(jnp.bfloat16), fresh_ref[:, :width]),
            )

            def absorb(k, carried, query=query, limit=limit):
                top, total, weighted = carried
                base = pl.multiple_of(k * chunk, chunk)
                scores = cache_scores(query, limit, base, chunk)
                new_top = jnp.maximum(top, jnp.max(scores, axis=-1, keepdims=True))
                weights = weights_of(scores, new_top)
                factor = weights_of(top, new_top)
                total = total * factor + jnp.sum(weights, axis=-1, keepdims=True)
                weighted = weighted * factor + dot_nn(
                    weights.astype(jnp.bfloat16), lat_ref[pl.ds(base, chunk), :width]
                )
                return new_top, total, weighted

            top, total, weighted = lax.fori_loop(0, n_keys // chunk, absorb, state)
        store(i, weighted, total)


def decode(q, gathered, new_raw, gain, owner, decode_len):
    n_steps, r_all, heads, full = q.shape
    width = gain.shape[1]
    n_new = -(-(n_steps * r_all) // BLK) * BLK
    r_here = r_all
    return pl.pallas_call(
        functools.partial(decode_kernel, width=width),
        grid=(n_steps, r_all // r_here),
        out_shape=(
            jax.ShapeDtypeStruct((n_steps, r_all, heads, width), jnp.bfloat16),
            jax.ShapeDtypeStruct((CAP, BLK, full), jnp.bfloat16),
        ),
        in_specs=[
            pl.BlockSpec(memory_space=pltpu.SMEM),
            pl.BlockSpec(memory_space=pltpu.SMEM),
            pl.BlockSpec((1, r_here, heads, full), lambda s, r: (s, r, 0, 0)),
            pl.BlockSpec(gathered.shape, lambda s, r: (0, 0)),
            pl.BlockSpec(new_raw.shape, lambda s, r: (0, 0, 0)),
            pl.BlockSpec(gain.shape, lambda s, r: (0, 0)),
        ],
        out_specs=(
            pl.BlockSpec((1, r_here, heads, width), lambda s, r: (s, r, 0, 0)),
            pl.BlockSpec((CAP, BLK, full), lambda s, r: (0, 0, 0)),
        ),
        scratch_shapes=[pltpu.VMEM((n_new, full), jnp.bfloat16)],
        compiler_params=pltpu.CompilerParams(vmem_limit_bytes=VMEM_LIMIT),
        name="decode",
    )(owner, decode_len, q, gathered, new_raw, gain)


def gather(kv_raw, gain):
    row_count, full = kv_raw.shape
    me = lax.axis_index("ctx")
    positions = me * row_count + jnp.arange(row_count, dtype=jnp.int32)
    freq = frequencies((full - gain.shape[1]) // 2)
    latent = normalize_rows(kv_raw, gain, positions[:, None], freq)
    return lax.all_gather(latent, "ctx", axis=0, tiled=True)


def body(q_prefill, kv_raw, kv_gain, block_mask, owner, decode_len, q_decode, kv_new_raw):
    gain = kv_gain.reshape(1, -1)
    gathered = gather(kv_raw, gain)
    prefill_out = prefill(q_prefill, gathered, block_mask, gain.shape[1])
    decode_out, owner_cache = decode(q_decode, gathered, kv_new_raw, gain, owner, decode_len)
    return (prefill_out, owner_cache, decode_out)


def solution(mesh):
    return jax.shard_map(
        body,
        mesh=mesh,
        in_specs=(
            P(("groups", "ctx"), "head", None),
            P(("groups", "ctx"), None),
            P(),
            P("groups", None),
            P("groups"),
            P("groups"),
            P(None, "groups", "head", None),
            P(None, "groups", None),
        ),
        out_specs=(
            P(("groups", "ctx"), "head", None),
            P(("groups", "ctx"), None, None),
            P(None, "groups", "head", None),
        ),
        check_vma=False,
    )
```

time: 260 us -> 83.9 us (0.32)
  the two profiles are of different devices: /device:TPU:2 before, /device:TPU:30 now
where the time goes in v1:
time: 83.9 us; the launch traced here: 83.2 us
  waiting for transfers between devices  32.2 us (38%)
  Pallas kernels  23 us (27%)
  between operations  14.1 us (17%)
  local copies, waits for them, and re-layouts  11.9 us (14%)
  other arithmetic  2 us (2%)
    all_gather x1, waiting for transfers between devices, gather(): return lax.all_gather(latent, 'ctx', axis=0, tiled=True)  32.2 us
    pallas_call x1, Pallas kernels, prefill(): pl.pallas_call(functools.partial(prefill_kernel, n_blocks=n_blocks, width...  12.8 us
    unnamed x3, local copies, waits for them, and re-layouts  11.9 us
    pallas_call x1, Pallas kernels, decode(): pl.pallas_call(functools.partial(decode_kernel, width=width), grid=(n_ste...  10.2 us
  transfers between devices with their start and end apart: 1, of which 1 were waited for; matrix products, arithmetic and copies ran while one was open for 11% of the time, Pallas kernels for 0%

profile of v1, /device:TPU:30, one launch (start us, length us, event | category | flops | bytes accessed | tf_op | source)
XLA Modules:
  0.0 83.2 jit_solution(9361788873280206695)
XLA Ops:
  7.2 0.0 all-gather.2.cloned.1.call-start
  7.2 1.1 %copy.14 = bf16[128,576]{1,0:T(8,128)(2,1)S(1)} copy(bf16[128,576]{0,1:T(8,128)(2,1)} %param.9) | data formatting | bytes 294912 | tf_op args[1]
  8.3 0.1 multiply_reduce_fusion
  8.5 0.3 fusion.5
  8.8 0.8 multiply_convert_fusion
  9.6 0.8 pad_maximum_fusion
  10.3 0.0 all-gather.2.cloned.1.call-update
  10.4 9.0 %copy.16.q_ref = bf16[128,32,576]{2,1,0:T(8,128)(2,1)} copy(bf16[128,32,576]{0,2,1:T(8,128)(2,1)} %param.8) | data formatting | bytes 9437184 | tf_op args[0]
  19.3 32.2 %all-gather.2.cloned.1.call-done.lat_ref = bf16[1024,576]{1,0:T(8,128)(2,1)} async-done(((bf16[128,576]{1,0:T(8,128)(2,1)}), bf16[1024,576]{1,0:T(8,128)(2,1)}) %all-gather.2.cloned.1.call-update) | async-done | bytes 1179664 | tf_op jit(solution)/shard_map/all_gather | solution.py:339
  51.5 10.2 %decode.1 = (bf16[3,16,32,512]{3,2,1,0:T(8,128)(2,1)}, bf16[2,128,576]{2,1,0:T(8,128)(2,1)}) custom-call(s32[8]{0:T(128)} %owner_ref.1, s32[16]{0:T(128)} %len_ref.1, bf16[3,16,32,576]{3,2,1,0:T(8,128)(2,1)} %q_ref.2, bf16[1024,576]{1,0:T(8,128)(2,1)} %all-gather.2.cloned.1.call-done.lat_ref, bf16[3,16,576]{2,1,0:T(8,128)(2,1)} %new_ref.1, f32[1,512]{1,0:T(1,128)} %bitcast.1), custom_call_target="tpu_custom_call" | custom-call | tf_op jit(solution)/shard_map/decode/pallas_call | solution.py:308
  61.7 1.9 %copy.17 = bf16[2,128,576]{1,2,0:T(8,128)(2,1)} copy(bf16[2,128,576]{2,1,0:T(8,128)(2,1)} %get-tuple-element.11) | data formatting | bytes 589824
  63.5 12.8 %prefill.1 = bf16[128,32,512]{2,1,0:T(8,128)(2,1)} custom-call(s32[8,8]{1,0:T(8,128)} %mask_ref.1, bf16[128,32,576]{2,1,0:T(8,128)(2,1)} %copy.16.q_ref, bf16[1024,576]{1,0:T(8,128)(2,1)} %all-gather.2.cloned.1.call-done.lat_ref), custom_call_target="tpu_custom_call" | custom-call | tf_op jit(solution)/shard_map/prefill/pallas_call | solution.py:171
  (4 shorter events, 0.0 us)
Async XLA Ops:
  7.2 44.3 %all-gather.2.cloned.1.call-start = ((), (), s32[]{:S(2)}) async-start(), calls=%async_computation | async-start | bytes 1474560 | tf_op jit(solution)/shard_map/all_gather | solution.py:339
Sparse Core Ops, SparseCore 0:
  10.8 40.6 all-gather.1
